TPU v7x, 32 devices: a whole 2x2x4 slice. The times are simulated.
32 devices in a mesh: seq: 8 (over z, y), tp: 4 (over x, core).
Axes of the slice: x: 2, y: 2, z: 4, core: 2. Of those that a mesh axis runs over, the one named last changes fastest.
Arguments:
- hidden_in: bfloat16 [16, 1024, 2048], P('seq', None, 'tp'), may hold values from -6 to 6
- cotangent: bfloat16 [16, 1024, 2048], P('seq', None, 'tp'), may hold values from -6 to 6
- token_mask: int32 [16, 1024], P('seq'), may hold values 0 or 1
- w_qkv: bfloat16 [2048, 3, 16, 128], P(None, None, 'tp'), may hold values from -0.125 to 0.125
- w_out: bfloat16 [16, 128, 2048], P('tp'), may hold values from -0.125 to 0.125
- time_bias: float32 [16, 16, 16], P('tp'), may hold values from -2 to 252
Outputs:
- grad_input: bfloat16 [16, 1024, 2048], P('seq', None, 'tp')
- grad_qkv: float32 [2048, 3, 16, 128], P('seq', None, 'tp')
- grad_out: float32 [16, 128, 2048], P('tp', None, 'seq')
All inputs are finite; a program needn't handle non-finite values. No bound on the sum of `token_mask` on one device may be relied on, other than what follows from the above.
Results may differ from a plain program's by a relative error of at most 0.012.
The roundings to bfloat16 on the way count: a program that leaves them out, or rounds other values in their place, can miss the bound.
Values may be sent and summed in bfloat16 or wider, within the bound.
No kernel may reach another device: no remote copies, remote signals or barrier semaphores. Data moves between devices by JAX's collectives and lax.ppermute only.
A program may use at most 192 MiB of HBM per device.

v0:
```python
import math

import jax
import jax.numpy as jnp
from jax import lax
from jax.sharding import PartitionSpec as P

TOKENS = 16384


def on_device(hidden_in, cotangent, token_mask, w_qkv, w_out, time_bias):
    masked = cotangent * token_mask[:, :, None].astype(jnp.bfloat16)
    rows_in, rows_grad = (
        lax.all_to_all(hidden_in, "seq", split_axis=1, concat_axis=0, tiled=True),
        lax.all_to_all(masked, "seq", split_axis=1, concat_axis=0, tiled=True),
    )
    full_in, full_grad = (
        lax.all_gather(rows_in, "tp", axis=2, tiled=True),
        lax.all_gather(rows_grad, "tp", axis=2, tiled=True),
    )
    frames, places, width = full_in.shape
    count = frames * places
    local_heads = w_qkv.shape[2]
    head_size = w_qkv.shape[3]
    scale = 1.0 / math.sqrt(head_size)
    root = math.sqrt(TOKENS)
    flat_in = full_in.reshape(count, width)
    flat_grad = full_grad.reshape(count, width)
    proj = w_qkv.reshape(width, 3 * local_heads * head_size)
    qkv = jnp.dot(flat_in, proj, preferred_element_type=jnp.float32).astype(jnp.bfloat16)
    qkv = qkv.reshape(frames, places, 3, local_heads, head_size)
    query, keys, values = (qkv[:, :, 0], qkv[:, :, 1], qkv[:, :, 2])
    scores = jnp.einsum("fphd,gphd->phfg", query, keys, preferred_element_type=jnp.float32) * scale
    scores = scores + time_bias[None]
    probs = jax.nn.softmax(scores, axis=-1)
    probs_low = probs.astype(jnp.bfloat16)
    attn = jnp.einsum(
        "phfg,gphd->fphd", probs_low, values, preferred_element_type=jnp.float32
    ).astype(jnp.bfloat16)
    out_proj = w_out.reshape(local_heads * head_size, width)
    d_attn = lax.dot_general(
        flat_grad, out_proj, (((1,), (1,)), ((), ())), preferred_element_type=jnp.float32
    ).astype(jnp.bfloat16)
    out_grad = (
        lax.dot_general(
            attn.reshape(count, local_heads * head_size),
            flat_grad,
            (((0,), (0,)), ((), ())),
            preferred_element_type=jnp.float32,
        )
        / root
    )
    d_attn4 = d_attn.reshape(frames, places, local_heads, head_size)
    d_values = jnp.einsum("phfg,fphd->gphd", probs_low, d_attn4, preferred_element_type=jnp.float32)
    d_probs = jnp.einsum("fphd,gphd->phfg", d_attn4, values, preferred_element_type=jnp.float32)
    d_scores = probs * (d_probs - jnp.sum(probs * d_probs, axis=-1, keepdims=True))
    d_scores = d_scores.astype(jnp.bfloat16)
    d_query = (
        jnp.einsum("phfg,gphd->fphd", d_scores, keys, preferred_element_type=jnp.float32) * scale
    )
    d_keys = (
        jnp.einsum("phfg,fphd->gphd", d_scores, query, preferred_element_type=jnp.float32) * scale
    )
    d_qkv = (
        jnp.stack([d_query, d_keys, d_values], axis=2)
        .astype(jnp.bfloat16)
        .reshape(count, 3 * local_heads * head_size)
    )
    qkv_grad = (
        lax.dot_general(
            flat_in, d_qkv, (((0,), (0,)), ((), ())), preferred_element_type=jnp.float32
        )
        / root
    )
    partial_value = lax.dot_general(
        d_qkv, proj, (((1,), (1,)), ((), ())), preferred_element_type=jnp.float32
    ).reshape(frames, places, width)
    summed = lax.psum_scatter(partial_value, "tp", scatter_dimension=2, tiled=True).astype(
        jnp.bfloat16
    )
    grad_input = lax.all_to_all(summed, "seq", split_axis=0, concat_axis=1, tiled=True)
    joined = jnp.concatenate([qkv_grad, out_grad.T], axis=1)
    summed_both = lax.psum_scatter(joined, "seq", scatter_dimension=0, tiled=True)
    qkv_sum = summed_both[:, : 3 * local_heads * head_size]
    out_sum = summed_both[:, 3 * local_heads * head_size :].T.reshape(
        local_heads, head_size, summed_both.shape[0]
    )
    grad_qkv = qkv_sum.reshape(qkv_sum.shape[0], 3, local_heads, head_size)
    return (grad_input, grad_qkv, out_sum)


def solution(mesh):
    in_specs = (
        P("seq", None, "tp"),
        P("seq", None, "tp"),
        P("seq", None),
        P(None, None, "tp", None),
        P("tp", None, None),
        P("tp", None, None),
    )
    out_specs = (P("seq", None, "tp"), P("seq", None, "tp", None), P("tp", None, "seq"))
    return jax.shard_map(
        on_device, mesh=mesh, in_specs=in_specs, out_specs=out_specs, check_vma=False
    )
```

profile of v0, /device:TPU:0, one launch (start us, length us, event | category | flops | bytes accessed | tf_op | source)
XLA Modules:
  0.0 740.9 jit_solution(18426806565591482519)
XLA Ops:
  8.3 4.9 copy_multiply_fusion
  13.2 55.3 %all_to_all.54 = bf16[2,1024,512]{2,0,1:T(2,128)(2,1)S(1)} all-to-all(bf16[2,1024,512]{2,0,1:T(2,128)(2,1)S(1)} %copy_multiply_fusion), channel_id=1, replica_groups=mesh['seq'=8,'tp'=4] {'seq'}, dimensions={1} | all-to-all | bytes 4194304 | tf_op jit(solution)/shard_map/all_to_all | solution.py:15
  70.5 3.8 copy.51
  74.2 51.4 %all_to_all.55 = bf16[2,1024,512]{2,0,1:T(2,128)(2,1)S(1)} all-to-all(bf16[2,1024,512]{2,0,1:T(2,128)(2,1)S(1)} %copy.51), channel_id=1, replica_groups=mesh['seq'=8,'tp'=4] {'seq'}, dimensions={1} | all-to-all | bytes 4194304 | tf_op jit(solution)/shard_map/all_to_all | solution.py:14
  127.8 11.2 %reshape.53 = bf16[2048,1536]{1,0:T(8,128)(2,1)} reshape(bf16[2048,3,4,128]{3,2,1,0:T(4,128)(2,1)} %param.9) | data formatting | bytes 12582912 | tf_op jit(solution)/shard_map/reshape | solution.py:29
  138.9 10.5 %convolution_convert_fusion.1 = bf16[2048,512]{1,0:T(8,128)(2,1)} fusion(bf16[2048,2048]{1,0:T(8,128)(2,1)} %bitcast.92, bf16[512,2048]{1,0:T(8,128)(2,1)S(1)} %bitcast.82), kind=kOutput, calls=%fused_computation.19 | convolution fusion | flops 4296015872 | bytes 12582912 | tf_op jit(solution)/shard_map/dot_general | solution.py:41
  149.4 4.0 reshape.57
  153.4 34.4 %all-gather.3.cloned.1.call-done = bf16[16,128,2048]{2,1,0:T(8,128)(2,1)} async-done(((bf16[16,128,512]{2,1,0:T(8,128)(2,1)}), bf16[16,128,2048]{2,1,0:T(8,128)(2,1)}) %all-gather.3.cloned.1.call-update) | async-done | bytes 8388624 | tf_op jit(solution)/shard_map/all_gather | solution.py:18
  187.7 18.6 %convolution_convert_fusion = bf16[2048,1536]{1,0:T(8,128)(2,1)} fusion(bf16[2048,2048]{1,0:T(8,128)(2,1)} %bitcast.94, bf16[2048,1536]{1,0:T(8,128)(2,1)} %reshape.53), kind=kOutput, calls=%fused_computation.3 | convolution fusion | flops 12888047616 | bytes 20971520 | tf_op jit(solution)/shard_map/dot_general | solution.py:30
  206.3 11.3 %reshape.54 = bf16[16,128,3,4,128]{4,3,2,1,0:T(4,128)(2,1)} reshape(bf16[2048,1536]{1,0:T(8,128)(2,1)} %convolution_convert_fusion) | data formatting | bytes 12582912 | tf_op jit(solution)/shard_map/reshape | solution.py:31
  217.6 4.2 fusion.20
  221.9 2.5 fusion.11
  224.4 2.3 fusion.21
  226.8 1.6 convert_bitcast_fusion.1
  228.4 3.3 multiply_reduce_fusion
  234.5 1.7 fusion.15
  237.1 2.6 copy-done.2
  239.6 28.1 %convolution_bitcast_fusion = f32[16,128,2048]{2,1,0:T(8,128)} fusion(bf16[2048,3,4,128]{3,2,1,0:T(4,128)(2,1)} %param.9, bf16[16,128,3,4,128]{4,0,3,1,2:T(8,128)(2,1)S(1)} %pad_maximum_fusion.1), kind=kOutput, calls=%fused_computation.4 | convolution fusion | flops 12884901888 | bytes 29360128 | tf_op jit(solution)/shard_map/dot_general | solution.py:75
  267.8 10.2 %copy.68 = bf16[16,128,3,4,128]{1,0,4,3,2:T(8,128)(2,1)} copy(bf16[16,128,3,4,128]{4,0,3,1,2:T(8,128)(2,1)} %copy-done.2) | data formatting | bytes 12582912 | tf_op jit(solution)/shard_map/stack | solution.py:65
  277.9 5.9 convert_bitcast_fusion
  283.8 3.8 copy.70
  287.7 9.0 %convolution_multiply_fusion = f32[2048,512]{0,1:T(8,128)S(1)} fusion(bf16[2048,2048]{1,0:T(8,128)(2,1)} %bitcast.93, bf16[64,8,16,128]{3,2,1,0:T(8,128)(2,1)} %bitcast.90), kind=kOutput, calls=%fused_computation.17 | convolution fusion | flops 4296015872 | bytes 14680064 | tf_op jit(solution)/shard_map/dot_general | solution.py:45
  296.6 18.0 %multiply_bitcast_fusion = f32[2048,1536]{0,1:T(8,128)S(1)} fusion(bf16[2048,2048]{1,0:T(8,128)(2,1)} %bitcast.95, bf16[192,8,16,128]{3,2,1,0:T(8,128)(2,1)} %bitcast.87), kind=kOutput, calls=%fused_computation.2 | convolution fusion | flops 12888047616 | bytes 27262976 | tf_op jit(solution)/shard_map/dot_general | solution.py:70
  314.6 6.3 pad_maximum_fusion
  320.9 73.1 %reduce-scatter.3.cloned.1.call-done = f32[16,128,512]{2,1,0:T(8,128)} async-done(((f32[16,128,2048]{2,1,0:T(8,128)}), f32[16,128,512]{2,1,0:T(8,128)}) %reduce-scatter.3.cloned.1.call-update) | async-done | bytes 4194320 | tf_op jit(solution)/shard_map/reduce_scatter | solution.py:78
  394.0 3.8 convert_element_type.43
  397.8 5.5 all-to-all-start.2
  403.3 320.5 %reduce-scatter.5.cloned.1.call-done = f32[256,2048]{0,1:T(8,128)} async-done(((f32[2048,2048]{0,1:T(8,128)}), f32[256,2048]{0,1:T(8,128)}) %reduce-scatter.5.cloned.1.call-update) | async-done | bytes 2097168 | tf_op jit(solution)/shard_map/reduce_scatter | solution.py:83
  723.8 2.7 slice.23
  726.5 2.7 copy.71
  729.2 1.9 slice.24
  731.1 3.1 copy.67
  (33 shorter events, 8.9 us)
Async XLA Ops:
  7.2 131.8 %copy-start = (bf16[4,128,2048]{2,1,0:T(8,128)(2,1)S(1)}, bf16[4,128,2048]{2,1,0:T(8,128)(2,1)}, u32[]{:S(2)}) copy-start(bf16[4,128,2048]{2,1,0:T(8,128)(2,1)} %param.10) | copy-start | bytes 6291460
  7.2 131.8 %all-gather.5.cloned.1.call-start = ((), (), s32[]{:S(2)}) async-start(), calls=%async_computation.6 | async-start | bytes 10485760 | tf_op jit(solution)/shard_map/all_gather | solution.py:19
  70.4 117.3 %all-gather.3.cloned.1.call-start = ((), (), s32[]{:S(2)}) async-start(), calls=%async_computation.5 | async-start | bytes 10485760 | tf_op jit(solution)/shard_map/all_gather | solution.py:18
  125.9 1.8 copy-start.6
  127.5 266.5 %reduce-scatter.3.cloned.1.call-start = ((), (), s32[]{:S(2)}) async-start(), calls=%async_computation.7 | async-start | bytes 20971520 | tf_op jit(solution)/shard_map/reduce_scatter | solution.py:78
  221.9 6.5 copy-start.5
  224.4 2.3 copy-start.4
  226.7 4.9 copy-start.3
  237.1 2.6 copy-start.2
  267.7 456.1 %reduce-scatter.5.cloned.1.call-start = ((), (), s32[]{:S(2)}) async-start(), calls=%async_computation.8 | async-start | bytes 18874368 | tf_op jit(solution)/shard_map/reduce_scatter | solution.py:83
  397.8 333.3 %all-to-all-start.2 = ((bf16[16,128,512]{2,1,0:T(8,128)(2,1)}), bf16[16,128,512]{2,1,0:T(8,128)(2,1)}, u32[]{:S(2)}, u32[]{:S(2)}) async-start(bf16[16,128,512]{2,1,0:T(8,128)(2,1)} %convert_element_type.43), calls=%async_computation.3 | async-start | bytes 4194304 | tf_op jit(solution)/shard_map/all_to_all | solution.py:81
  726.5 7.7 %copy-start.1 = (bf16[4,128,2048]{2,1,0:T(8,128)(2,1)S(1)}, bf16[4,128,2048]{2,1,0:T(8,128)(2,1)}, u32[]{:S(2)}) copy-start(bf16[4,128,2048]{2,1,0:T(8,128)(2,1)} %param.10) | copy-start | bytes 6291460
Sparse Core Ops, SparseCore 0:
  70.5 57.2 all-gather.4
  129.4 58.2 all-gather.2
  267.8 126.1 reduce-scatter.2
  398.1 325.6 reduce-scatter.4
where the time goes:
time: 746 us; the launch traced here: 741 us
  waiting for transfers between devices  428 us (57%)
  blocking collectives  107 us (14%)
  matrix products  101 us (14%)
  local copies, waits for them, and re-layouts  65.3 us (9%)
  other arithmetic  20.2 us (3%)
  between operations  14.1 us (2%)
    reduce_scatter x1, waiting for transfers between devices, on_device(): lax.psum_scatter(joined, 'seq', scatter_dimension=0, tiled=True)  321 us
    reduce_scatter x1, waiting for transfers between devices, on_device(): lax.psum_scatter(partial_value, 'tp', scatter_dimension=2, tiled=True)  73.1 us
    all_to_all x1, blocking collectives, on_device(): lax.all_to_all(masked, 'seq', split_axis=1, concat_axis=0, tiled=True)  55.3 us
    all_to_all x1, blocking collectives, on_device(): lax.all_to_all(hidden_in, 'seq', split_axis=1, concat_axis=0, tiled=True)  51.4 us
    all_gather x1, waiting for transfers between devices, on_device(): lax.all_gather(rows_in, 'tp', axis=2, tiled=True)  34.4 us
    dot_general x1, matrix products, on_device(): lax.dot_general(d_qkv, proj, (((1,), (1,)), ((), ())), preferred_element_...  28.1 us
    dot_general x1, matrix products, on_device(): jnp.dot(flat_in, proj, preferred_element_type=jnp.float32)  18.6 us
    dot_general x1, matrix products, on_device(): lax.dot_general(flat_in, d_qkv, (((0,), (0,)), ((), ())), preferred_eleme...  18 us
  transfers between devices with their start and end apart: 5, of which 3 were waited for; matrix products, arithmetic and copies ran while one was open for 13% of the time, Pallas kernels for 0%

commit v1 on v0

v1 whole, which is shorter than its diff:
```python
import functools
import math

import jax
import jax.numpy as jnp
from jax import lax
from jax.experimental import pallas as pl
from jax.experimental.pallas import tpu as pltpu
from jax.sharding import PartitionSpec as P

BF = jnp.bfloat16
F32 = jnp.float32
STEP = 16
MIB = 1 << 20


def xor_pairs(size, bit):
    return [(i, i ^ bit) for i in range(size)]


def dot(a, b, dims):
    return lax.dot_general(a, b, ((dims[0], dims[1]), ((), ())), preferred_element_type=F32)


def pack_kernel(h_ref, c_ref, m_ref, o_ref):
    for f in range(h_ref.shape[0]):
        o_ref[:, 0, f] = h_ref[f]
        o_ref[:, 1, f] = c_ref[f] * m_ref[f]


def pack(hidden, cot, mask, first, count):
    frames, seq, _, width = hidden.shape
    off = first // STEP
    data = pl.BlockSpec((frames, seq, STEP, width), lambda i: (0, 0, off + i, 0))
    return pl.pallas_call(
        pack_kernel,
        grid=(count // STEP,),
        in_specs=[data, data, pl.BlockSpec((frames, seq, STEP, 1), lambda i: (0, 0, off + i, 0))],
        out_specs=pl.BlockSpec((seq, 2, frames, STEP, width), lambda i: (0, 0, 0, i, 0)),
        out_shape=jax.ShapeDtypeStruct((seq, 2, frames, count, width), BF),
        compiler_params=pltpu.CompilerParams(vmem_limit_bytes=32 * MIB),
        cost_estimate=pl.CostEstimate(
            flops=0, bytes_accessed=8 * frames * seq * count * width, transcendentals=0
        ),
    )(hidden, cot, mask)


def layer_kernel(tp, heads, n_alias, where_ref, *refs):
    pieces = refs[:tp]
    w_ref, wt_ref, wo_ref, bias_ref = refs[tp : tp + 4]
    x_ref, g_ref, dqkv_ref, attn_ref, keep_ref, send_ref = refs[tp + 4 + n_alias : tp + 10 + n_alias]
    qkv_ref, da_ref = refs[tp + 10 + n_alias :]
    me, parity = where_ref[0], where_ref[1]
    rows = x_ref.shape[1]
    part = wt_ref.shape[1] // tp
    seq = pieces[0].shape[0]
    unit = wt_ref.shape[1] // seq
    head = bias_ref.shape[1]
    size = qkv_ref.shape[1] // (3 * heads)
    scale = 1.0 / math.sqrt(size)
    for j in range(tp):
        block = me ^ j
        for i in range(part // unit):
            dest = block * (part // unit) + i
            side = jnp.where(dest % 2 == parity, 1, 0)
            cols = pl.ds(pl.multiple_of((dest // 2) * unit, unit), unit)
            lanes = slice(i * unit, (i + 1) * unit)
            x_ref[side, :, cols] = pieces[j][:, 0, :, :, lanes].reshape(rows, unit)
            g_ref[side, :, cols] = pieces[j][:, 1, :, :, lanes].reshape(rows, unit)
    da_ref[...] = (
        dot(g_ref[0], wo_ref[0], ((1,), (0,))) + dot(g_ref[1], wo_ref[1], ((1,), (0,)))
    ).astype(BF)
    qkv_ref[...] = (
        dot(x_ref[0], w_ref[0], ((1,), (0,))) + dot(x_ref[1], w_ref[1], ((1,), (0,)))
    ).astype(BF)
    for h in range(heads):
        at = [slice((c * heads + h) * size, (c * heads + h + 1) * size) for c in range(3)]
        q, k, v = (qkv_ref[:, a] for a in at)
        da = da_ref[:, at[0]]
        s = dot(q, k, ((1,), (1,))) * scale + bias_ref[h]
        e = jnp.exp(s - jnp.max(s, axis=1, keepdims=True))
        p = e / jnp.sum(e, axis=1, keepdims=True)
        low = p.astype(BF)
        attn_ref[:, at[0]] = dot(low, v, ((1,), (0,))).astype(BF)
        dqkv_ref[:, at[2]] = dot(low, da, ((0,), (0,))).astype(BF)
        dp = dot(da, v, ((1,), (1,)))
        ds = (p * (dp - jnp.sum(p * dp, axis=1, keepdims=True))).astype(BF)
        dqkv_ref[:, at[0]] = (dot(ds, k, ((1,), (0,))) * scale).astype(BF)
        dqkv_ref[:, at[1]] = (dot(ds, q, ((0,), (0,))) * scale).astype(BF)
    grad = dqkv_ref[...]
    for j in range(tp):
        cols = pl.ds(pl.multiple_of((me ^ j) * part, part), part)
        out = send_ref if j % 2 else keep_ref
        val = dot(grad, wt_ref[:, cols], ((1,), (0,)))
        out[j // 2] = val.astype(out.dtype).reshape(out.shape[1:])


def layer(where, pieces, weights, carried, first, total):
    w2, wt, wo2, bias = weights
    tp = len(pieces)
    seq, _, frames, count, part = pieces[0].shape
    width = part * tp
    rows = seq * frames * STEP
    heads = bias.shape[0]
    cols = w2.shape[2]
    model = cols // 3
    off = first // STEP
    tokens = seq * frames * total
    piece = pl.BlockSpec((seq, 2, frames, STEP, part), lambda i, s: (0, 0, 0, i, 0))

    def whole(a):
        return pl.BlockSpec(a.shape, lambda i, s: (0,) * a.ndim, pipeline_mode=pl.Buffered(1))

    half = pl.BlockSpec((2, rows, width // 2), lambda i, s: (0, off + i, 0))

    def line(n):
        return pl.BlockSpec((rows, n), lambda i, s: (off + i, 0))

    back = pl.BlockSpec((tp // 2, seq, frames, STEP, part), lambda i, s: (0, 0, 0, i, 0))
    sds = jax.ShapeDtypeStruct
    n_alias = len(carried)
    work = seq * frames * count
    return pl.pallas_call(
        functools.partial(layer_kernel, tp, heads, n_alias),
        grid_spec=pltpu.PrefetchScalarGridSpec(
            num_scalar_prefetch=1,
            grid=(count // STEP,),
            in_specs=[piece] * tp
            + [whole(a) for a in weights]
            + [pl.BlockSpec(memory_space=pl.ANY)] * n_alias,
            out_specs=[half, half, line(cols), line(model), back, back],
            scratch_shapes=[pltpu.VMEM((rows, cols), BF), pltpu.VMEM((rows, model), BF)],
        ),
        out_shape=[
            sds((2, tokens, width // 2), BF),
            sds((2, tokens, width // 2), BF),
            sds((tokens, cols), BF),
            sds((tokens, model), BF),
            sds((tp // 2, seq, frames, count, part), F32),
            sds((tp // 2, seq, frames, count, part), BF),
        ],
        input_output_aliases={1 + tp + 4 + i: i for i in range(n_alias)},
        compiler_params=pltpu.CompilerParams(vmem_limit_bytes=56 * MIB),
        cost_estimate=pl.CostEstimate(
            flops=2 * work * width * cols * 7 // 3,
            bytes_accessed=14 * MIB + work * width * 12,
            transcendentals=work * rows * heads,
        ),
    )(where, *pieces, *weights, *carried)


def chunks_of(total):
    units = total // STEP
    if units < 4:
        return [STEP] * units
    last = max(1, units // 4)
    a = (units - last + 1) // 2
    return [n * STEP for n in (a, units - last - a, last)]


def exchange_seq(a):
    return lax.all_to_all(a, "seq", split_axis=0, concat_axis=0, tiled=True)


def on_device(seq, tp, hidden_in, cotangent, token_mask, w_qkv, w_out, time_bias):
    frames, places, part = hidden_in.shape
    width = part * tp
    total = places // seq
    heads, size = w_out.shape[0], w_out.shape[1]
    model = heads * size
    outer = seq // 2
    unit = width // seq
    me_s, me_t = lax.axis_index("seq"), lax.axis_index("tp")
    z, y = me_s // 2, me_s % 2
    where = jnp.stack([me_t, y]).astype(jnp.int32)
    root = math.sqrt(seq * frames * places)

    hidden = hidden_in.reshape(frames, seq, total, part)
    cot = cotangent.reshape(frames, seq, total, part)
    mask = token_mask.astype(BF).reshape(frames, seq, total, 1)
    sizes = chunks_of(total)
    starts = [sum(sizes[:k]) for k in range(len(sizes))]
    packed = [pack(hidden, cot, mask, a, n) for a, n in zip(starts, sizes)]

    proj = w_qkv.reshape(width, 3 * model)
    proj_t = proj.T
    out_t = w_out.reshape(model, width).T

    def sides(a):
        a = a.reshape(outer, 2, unit, a.shape[-1])
        pick = [lax.dynamic_index_in_dim(a, i, 1, False) for i in (1 - y, y)]
        return jnp.stack([p.reshape(width // 2, a.shape[-1]) for p in pick])

    place = jnp.arange(STEP)
    same = (place[:, None] == place[None, :])[None, None, :, None, :]
    bias = jnp.where(same, time_bias[:, :, None, :, None], -1e30)
    step_rows = seq * frames * STEP
    weights = (sides(proj), proj_t, sides(out_t), bias.reshape(heads, step_rows, step_rows))

    carried = []
    arrived, outs = [], []
    for k, (a, n) in enumerate(zip(starts, sizes)):
        block = packed[k]
        if k >= 2:
            block, arrived[k - 2] = lax.optimization_barrier((block, arrived[k - 2]))
        block = exchange_seq(block)
        pieces = {0: block}
        bit = tp // 2
        while bit:
            for j in list(pieces):
                pieces[j ^ bit] = lax.ppermute(pieces[j], "tp", xor_pairs(tp, bit))
            bit //= 2
        arrived.append([pieces[j] for j in range(tp)])
    for k, (a, n) in enumerate(zip(starts, sizes)):
        res = layer(where, arrived[k], weights, carried, a, total)
        carried = res[:4]
        keep, send = res[4:]
        bit = 1
        while True:
            got = lax.ppermute(send, "tp", xor_pairs(tp, bit))
            both = keep.astype(F32) + got.astype(F32)
            bit *= 2
            if bit >= tp:
                break
            keep, send = both[0::2], both[1::2].astype(BF)
        outs.append(exchange_seq(both[0].astype(BF)))
    x2, g2, dqkv, attn = carried

    def summed(lhs, rhs):
        def rows_of(side):
            return dot(lhs[side], rhs, ((0,), (0,))).astype(BF)

        got = lax.ppermute(rows_of(0), "seq", xor_pairs(seq, 1))
        both = (rows_of(1).astype(F32) + got.astype(F32)).astype(BF).reshape(outer, unit, rhs.shape[1])
        groups = [[2 * i + b for i in range(outer)] for b in range(2)]
        parts = lax.all_to_all(
            both, "seq", split_axis=0, concat_axis=0, tiled=True, axis_index_groups=groups
        )
        return jnp.sum(parts.astype(F32), axis=0) / root

    out_sum = summed(g2, attn).T.reshape(heads, size, unit)
    cols = [summed(x2, dqkv[:, c * model : (c + 1) * model]) for c in (2, 1, 0)]
    grad_qkv = jnp.concatenate(cols[::-1], axis=1).reshape(unit, 3, heads, size)
    grad_input = jnp.concatenate([jnp.swapaxes(o, 0, 1) for o in outs], axis=2).reshape(
        frames, places, part
    )
    return (grad_input, grad_qkv, out_sum)


def solution(mesh):
    in_specs = (
        P("seq", None, "tp"),
        P("seq", None, "tp"),
        P("seq", None),
        P(None, None, "tp", None),
        P("tp", None, None),
        P("tp", None, None),
    )
    out_specs = (P("seq", None, "tp"), P("seq", None, "tp", None), P("tp", None, "seq"))
    return jax.shard_map(
        functools.partial(on_device, mesh.shape["seq"], mesh.shape["tp"]),
        mesh=mesh,
        in_specs=in_specs,
        out_specs=out_specs,
        check_vma=False,
    )
```

time: 746 us -> 473 us (0.63)
  waiting for transfers between devices: 428 us -> 190 us
  blocking collectives: 107 us -> 0 us
  Pallas kernels: 0 us -> 85.9 us
  matrix products: 101 us -> 40.4 us
  starting transfers between devices: 5.85 us -> 63.9 us
  between operations: 14.1 us -> 1.56 us
  local copies, waits for them, and re-layouts: 65.3 us -> 53.8 us
  other arithmetic: 20.2 us -> 29.4 us
    reduce_scatter x2 -> x0, waiting for transfers between devices: 394 us -> none  [the longest x1 321 us: on_device(): lax.psum_scatter(joined, 'seq', scatter_dimension=0, tiled=True)]
    all_to_all x2 -> x0, blocking collectives: 107 us -> none  [the longest x1 55.3 us: on_device(): lax.all_to_all(masked, 'seq', split_axis=1, concat_axis=0, tiled=True)]
    ppermute x0 -> x19, waiting for transfers between devices: none -> 104 us  [the longest x4 62.2 us: summed(): got = lax.ppermute(rows_of(0), 'seq', xor_pairs(seq, 1))]
    all_to_all x1 -> x10, waiting for transfers between devices: 0.01 us -> 86.7 us  [the longest x6 72.2 us: exchange_seq(): return lax.all_to_all(a, 'seq', split_axis=0, concat_axis=0, tiled=True)]
    pallas_call x0 -> x6, Pallas kernels: none -> 85.9 us  [the longest x3 83.4 us: layer(): pl.pallas_call(functools.partial(layer_kernel, tp, heads, n_alias), grid_...]
    dot_general x11 -> x8, matrix products: 101 us -> 40.4 us  [dot(): lax.dot_general(a, b, ((dims[0], dims[1]), ((), ())), preferred_element_t...]
    all_to_all x1 -> x10, starting transfers between devices: 5.52 us -> 51.6 us  [the longest x6 32.3 us: exchange_seq(): return lax.all_to_all(a, 'seq', split_axis=0, concat_axis=0, tiled=True)]
    all_gather x2 -> x0, waiting for transfers between devices: 34.4 us -> none  [the longest x1 34.4 us: on_device(): lax.all_gather(rows_in, 'tp', axis=2, tiled=True)]
  transfers between devices with their start and end apart: 5 -> 29, of which waited for: 3 -> 11; matrix products, arithmetic and copies ran while one was open for 13% -> 23% of each run, Pallas kernels for 0% -> 18%
where the time goes in v1:
time: 473 us; the launch traced here: 465 us
  waiting for transfers between devices  190 us (40%)
  Pallas kernels  85.9 us (18%)
  starting transfers between devices  63.9 us (14%)
  local copies, waits for them, and re-layouts  53.8 us (11%)
  matrix products  40.4 us (9%)
  other arithmetic  29.4 us (6%)
    pallas_call x3, Pallas kernels, layer(): pl.pallas_call(functools.partial(layer_kernel, tp, heads, n_alias), grid_...  83.4 us
    all_to_all x6, waiting for transfers between devices, exchange_seq(): return lax.all_to_all(a, 'seq', split_axis=0, concat_axis=0, tiled=True)  72.2 us
    ppermute x4, waiting for transfers between devices, summed(): got = lax.ppermute(rows_of(0), 'seq', xor_pairs(seq, 1))  62.2 us
    dot_general x8, matrix products, dot(): lax.dot_general(a, b, ((dims[0], dims[1]), ((), ())), preferred_element_t...  40.4 us
    all_to_all x6, starting transfers between devices, exchange_seq(): return lax.all_to_all(a, 'seq', split_axis=0, concat_axis=0, tiled=True)  32.3 us
    ppermute x9, waiting for transfers between devices, on_device(): pieces[j ^ bit] = lax.ppermute(pieces[j], 'tp', xor_pairs(tp, bit))  22 us
    unnamed x40, local copies, waits for them, and re-layouts  22 us
    ppermute x6, waiting for transfers between devices, on_device(): got = lax.ppermute(send, 'tp', xor_pairs(tp, bit))  19.4 us
  transfers between devices with their start and end apart: 29, of which 11 were waited for; matrix products, arithmetic and copies ran while one was open for 23% of the time, Pallas kernels for 18%

profile of v1, /device:TPU:0, one launch (start us, length us, event | category | flops | bytes accessed | tf_op | source)
XLA Modules:
  0.0 465.3 jit_solution(6017401981919131248)
XLA Ops:
  7.3 7.4 %all-to-all-start = ((bf16[8,2,2,48,512]{4,3,2,1,0:T(8,128)(2,1)}), bf16[8,2,2,48,512]{4,3,2,1,0:T(8,128)(2,1)}, u32[]{:S(2)}, u32[]{:S(2)}) async-start(bf16[8,2,2,48,512]{4,3,2,1,0:T(8,128)(2,1)} %copy-done.6), calls=%async_computation | async-start | bytes 3145728 | tf_op jit(solution)/shard_map/all_to_all | solution.py:162
  18.1 33.7 %all-to-all-done.refs_0_ = bf16[8,2,2,48,512]{4,3,2,1,0:T(8,128)(2,1)} async-done(((bf16[8,2,2,48,512]{4,3,2,1,0:T(8,128)(2,1)}), bf16[8,2,2,48,512]{4,3,2,1,0:T(8,128)(2,1)}, u32[]{:S(2)}, u32[]{:S(2)}) %all-to-all-start) | async-done | bytes 1572896 | tf_op jit(solution)/shard_map/all_to_all | solution.py:162
  57.7 35.1 %all-to-all-done.2.refs_0_ = bf16[8,2,2,48,512]{4,3,2,1,0:T(8,128)(2,1)} async-done(((bf16[8,2,2,48,512]{4,3,2,1,0:T(8,128)(2,1)}), bf16[8,2,2,48,512]{4,3,2,1,0:T(8,128)(2,1)}, u32[]{:S(2)}, u32[]{:S(2)}) %all-to-all-start.2) | async-done | bytes 1572896 | tf_op jit(solution)/shard_map/all_to_all | solution.py:162
  97.1 10.6 %copy.38 = bf16[2048,3,4,128]{0,3,2,1:T(8,128)(2,1)} copy(bf16[2048,3,4,128]{3,2,1,0:T(4,128)(2,1)} %param.9) | data formatting | bytes 12582912 | tf_op args[3]
  107.8 11.1 %reshape_reshape.3 = bf16[4,2,256,1536]{3,2,1,0:T(8,128)(2,1)} reshape(bf16[2048,3,4,128]{3,2,1,0:T(4,128)(2,1)} %param.9) | data formatting | bytes 12582912 | tf_op jit(solution)/shard_map/reshape;reshape | solution.py:190
  126.6 6.2 %broadcast_in_dim.34 = f32[4,256,256]{2,1,0:T(8,128)S(1)} reshape(f32[4,16,16,16,16]{4,3,2,1,0:T(8,128)} %broadcast_in_dim.33) | data formatting | bytes 2097152 | tf_op jit(solution)/shard_map/jit(_where)/broadcast_in_dim | solution.py:196
  143.1 4.7 %all-to-all-start.4 = ((bf16[8,2,2,32,512]{4,3,2,1,0:T(8,128)(2,1)}), bf16[8,2,2,32,512]{4,3,2,1,0:T(8,128)(2,1)}, u32[]{:S(2)}, u32[]{:S(2)}) async-start(bf16[8,2,2,32,512]{4,3,2,1,0:T(8,128)(2,1)} %shard_map.85), calls=%async_computation.4 | async-start | bytes 2097152 | tf_op jit(solution)/shard_map/all_to_all | solution.py:162
  147.8 30.0 %shard_map.87 = (bf16[2,2048,1024]{2,1,0:T(8,128)(2,1)}, bf16[2,2048,1024]{2,1,0:T(8,128)(2,1)}, bf16[2048,1536]{1,0:T(8,128)(2,1)}, bf16[2048,512]{1,0:T(8,128)...) custom-call(s32[2]{0:T(128)} %pad_add_fusion.where_ref, ...), custom_call_target="tpu_custom_call" | custom-call | flops 11274289152 | bytes 33554432 | tf_op jit(solution)/shard_map/pallas_call | solution.py:123
  179.7 30.4 %shard_map.89 = (bf16[2,2048,1024]{2,1,0:T(8,128)(2,1)}, bf16[2,2048,1024]{2,1,0:T(8,128)(2,1)}, bf16[2048,1536]{1,0:T(8,128)(2,1)}, bf16[2048,512]{1,0:T(8,128)...) custom-call(s32[2]{0:T(128)} %pad_add_fusion.where_ref, ...), custom_call_target="tpu_custom_call", output_to_operand_aliasing={{0}: (9, {}), {1}: (10, {}), {2}: (11, {}), {3}: (12, {})} | custom-call | flops 11274289152 | bytes 33554432 | tf_op jit(solution)/shard_map/pallas_call | solution.py:123
  214.8 22.0 %collective-permute-done.11.refs_2_ = bf16[8,2,2,32,512]{4,3,2,1,0:T(8,128)(2,1)} collective-permute-done((bf16[8,2,2,32,512]{4,3,2,1,0:T(8,128)(2,1)}, bf16[8,2,2,32,512]{4,3,2,1,0:T(8,128)(2,1)}, u32[]{:S(2)}, u32[]{:S(2)}) %collective-permute-start.11) | collective-permute-done | bytes 1048608 | tf_op jit(solution)/shard_map/ppermute | solution.py:211
  240.4 13.2 %collective-permute-done.4 = bf16[1,8,2,48,512]{4,3,2,1,0:T(8,128)(2,1)S(1)} collective-permute-done((bf16[1,8,2,48,512]{4,3,2,1,0:T(8,128)(2,1)S(1)}, bf16[1,8,2,48,512]{4,3,2,1,0:T(8,128)(2,1)S(1)}, u32[]{:S(2)}, u32[]{:S(2)}) %collective-permute-start.4) | collective-permute-done | bytes 786464 | tf_op jit(solution)/shard_map/ppermute | solution.py:220
  254.7 6.0 %all-to-all-start.1 = ((bf16[8,2,48,512]{3,2,1,0:T(8,128)(2,1)}), bf16[8,2,48,512]{3,2,1,0:T(8,128)(2,1)}, u32[]{:S(2)}, u32[]{:S(2)}) async-start(bf16[8,2,48,512]{3,2,1,0:T(8,128)(2,1)} %fusion.69), calls=%async_computation.1 | async-start | bytes 1572864 | tf_op jit(solution)/shard_map/all_to_all | solution.py:162
  260.7 23.0 %shard_map.90 = (bf16[2,2048,1024]{2,1,0:T(8,128)(2,1)}, bf16[2,2048,1024]{2,1,0:T(8,128)(2,1)}, bf16[2048,1536]{1,0:T(8,128)(2,1)}, bf16[2048,512]{1,0:T(8,128)...) custom-call(s32[2]{0:T(128)} %pad_add_fusion.where_ref, ...), custom_call_target="tpu_custom_call", output_to_operand_aliasing={{0}: (9, {}), {1}: (10, {}), {2}: (11, {}), {3}: (12, {})} | custom-call | flops 7516192768 | bytes 27262976 | tf_op jit(solution)/shard_map/pallas_call | solution.py:123
  286.1 6.0 %all-to-all-start.3 = ((bf16[8,2,48,512]{3,2,1,0:T(8,128)(2,1)}), bf16[8,2,48,512]{3,2,1,0:T(8,128)(2,1)S(1)}, u32[]{:S(2)}, u32[]{:S(2)}) async-start(bf16[8,2,48,512]{3,2,1,0:T(8,128)(2,1)} %fusion.70), calls=%async_computation.3 | async-start | bytes 1572864 | tf_op jit(solution)/shard_map/all_to_all | solution.py:162
  295.0 5.2 %fusion.47 = bf16[1024,512]{1,0:T(8,128)(2,1)S(1)} fusion(bf16[2048,1536]{1,0:T(8,128)(2,1)} %get-tuple-element.46, bf16[2,2048,1024]{2,1,0:T(8,128)(2,1)} %get-tuple-element.45), kind=kOutput, calls=%fused_computation.54 | convolution fusion | flops 2148007936 | bytes 7340032 | tf_op jit(solution)/shard_map/dot_general | solution.py:22
  302.3 6.2 %collective-permute-done.14 = bf16[1,8,2,32,512]{4,3,2,1,0:T(8,128)(2,1)S(1)} collective-permute-done((bf16[1,8,2,32,512]{4,3,2,1,0:T(8,128)(2,1)S(1)}, bf16[1,8,2,32,512]{4,3,2,1,0:T(8,128)(2,1)S(1)}, u32[]{:S(2)}, u32[]{:S(2)}) %collective-permute-start.14) | collective-permute-done | bytes 524320 | tf_op jit(solution)/shard_map/ppermute | solution.py:220
  316.8 5.2 %fusion.32 = bf16[1024,512]{1,0:T(8,128)(2,1)S(1)} fusion(bf16[2048,1536]{1,0:T(8,128)(2,1)} %get-tuple-element.46, bf16[2,2048,1024]{2,1,0:T(8,128)(2,1)} %get-tuple-element.45), kind=kOutput, calls=%fused_computation.51 | convolution fusion | flops 2148007936 | bytes 7340032 | tf_op jit(solution)/shard_map/dot_general | solution.py:22
  322.0 10.5 %collective-permute-done.15 = bf16[1024,512]{1,0:T(8,128)(2,1)S(1)} collective-permute-done((bf16[1024,512]{1,0:T(8,128)(2,1)S(1)}, bf16[1024,512]{1,0:T(8,128)(2,1)S(1)}, u32[]{:S(2)}, u32[]{:S(2)}) %collective-permute-start.15) | collective-permute-done | bytes 1048608 | tf_op jit(solution)/shard_map/ppermute | solution.py:233
  333.8 4.7 %all-to-all-start.6 = ((bf16[4,256,512]{2,1,0:T(8,128)(2,1)}), bf16[4,256,512]{2,1,0:T(8,128)(2,1)S(1)}, u32[]{:S(2)}, u32[]{:S(2)}) async-start(bf16[4,256,512]{2,1,0:T(8,128)(2,1)} %bitcast.24), calls=%async_computation.6 | async-start | bytes 2097152 | tf_op jit(solution)/shard_map/all_to_all | solution.py:236
  338.5 5.2 %fusion.52 = bf16[1024,512]{1,0:T(8,128)(2,1)S(1)} fusion(bf16[2048,1536]{1,0:T(8,128)(2,1)} %get-tuple-element.46, bf16[2,2048,1024]{2,1,0:T(8,128)(2,1)} %get-tuple-element.45), kind=kOutput, calls=%fused_computation.55 | convolution fusion | flops 2148007936 | bytes 7340032 | tf_op jit(solution)/shard_map/dot_general | solution.py:22
  345.1 5.2 %fusion.37 = bf16[1024,512]{1,0:T(8,128)(2,1)S(1)} fusion(bf16[2048,1536]{1,0:T(8,128)(2,1)} %get-tuple-element.46, bf16[2,2048,1024]{2,1,0:T(8,128)(2,1)} %get-tuple-element.45), kind=kOutput, calls=%fused_computation.52 | convolution fusion | flops 2148007936 | bytes 7340032 | tf_op jit(solution)/shard_map/dot_general | solution.py:22
  350.3 17.8 %collective-permute-done.16 = bf16[1024,512]{1,0:T(8,128)(2,1)S(1)} collective-permute-done((bf16[1024,512]{1,0:T(8,128)(2,1)S(1)}, bf16[1024,512]{1,0:T(8,128)(2,1)S(1)}, u32[]{:S(2)}, u32[]{:S(2)}) %collective-permute-start.16) | collective-permute-done | bytes 1048608 | tf_op jit(solution)/shard_map/ppermute | solution.py:233
  369.4 4.8 %all-to-all-start.7 = ((bf16[4,256,512]{2,1,0:T(8,128)(2,1)}), bf16[4,256,512]{2,1,0:T(8,128)(2,1)}, u32[]{:S(2)}, u32[]{:S(2)}) async-start(bf16[4,256,512]{2,1,0:T(8,128)(2,1)} %bitcast.26), calls=%async_computation.7 | async-start | bytes 2097152 | tf_op jit(solution)/shard_map/all_to_all | solution.py:236
  374.2 5.2 %fusion.57 = bf16[1024,512]{1,0:T(8,128)(2,1)S(1)} fusion(bf16[2048,1536]{1,0:T(8,128)(2,1)} %get-tuple-element.46, bf16[2,2048,1024]{2,1,0:T(8,128)(2,1)} %get-tuple-element.45), kind=kOutput, calls=%fused_computation.56 | convolution fusion | flops 2148007936 | bytes 7340032 | tf_op jit(solution)/shard_map/dot_general | solution.py:22
  379.8 5.2 %fusion.42 = bf16[1024,512]{1,0:T(8,128)(2,1)S(1)} fusion(bf16[2048,1536]{1,0:T(8,128)(2,1)} %get-tuple-element.46, bf16[2,2048,1024]{2,1,0:T(8,128)(2,1)} %get-tuple-element.45), kind=kOutput, calls=%fused_computation.53 | convolution fusion | flops 2148007936 | bytes 7340032 | tf_op jit(solution)/shard_map/dot_general | solution.py:22
  385.0 17.4 %collective-permute-done.17 = bf16[1024,512]{1,0:T(8,128)(2,1)S(1)} collective-permute-done((bf16[1024,512]{1,0:T(8,128)(2,1)S(1)}, bf16[1024,512]{1,0:T(8,128)(2,1)S(1)}, u32[]{:S(2)}, u32[]{:S(2)}) %collective-permute-start.17) | collective-permute-done | bytes 1048608 | tf_op jit(solution)/shard_map/ppermute | solution.py:233
  403.7 5.1 %all-to-all-start.8 = ((bf16[4,256,512]{2,1,0:T(8,128)(2,1)}), bf16[4,256,512]{2,1,0:T(8,128)(2,1)}, u32[]{:S(2)}, u32[]{:S(2)}) async-start(bf16[4,256,512]{2,1,0:T(8,128)(2,1)} %bitcast.28), calls=%async_computation.8 | async-start | bytes 2097152 | tf_op jit(solution)/shard_map/all_to_all | solution.py:236
  408.8 4.6 fusion.65
  413.7 4.5 fusion.62
  418.2 16.6 %collective-permute-done.18 = bf16[1024,512]{1,0:T(8,128)(2,1)S(1)} collective-permute-done((bf16[1024,512]{1,0:T(8,128)(2,1)S(1)}, bf16[1024,512]{1,0:T(8,128)(2,1)S(1)}, u32[]{:S(2)}, u32[]{:S(2)}) %collective-permute-start.18) | collective-permute-done | bytes 1048608 | tf_op jit(solution)/shard_map/ppermute | solution.py:233
  436.1 4.8 %all-to-all-start.9 = ((bf16[4,256,512]{2,1,0:T(8,128)(2,1)}), bf16[4,256,512]{2,1,0:T(8,128)(2,1)S(1)}, u32[]{:S(2)}, u32[]{:S(2)}) async-start(bf16[4,256,512]{2,1,0:T(8,128)(2,1)} %bitcast.32), calls=%async_computation.9 | async-start | bytes 2097152 | tf_op jit(solution)/shard_map/all_to_all | solution.py:236
  447.7 14.5 %all-to-all-done.9 = bf16[4,256,512]{2,1,0:T(8,128)(2,1)S(1)} async-done(((bf16[4,256,512]{2,1,0:T(8,128)(2,1)}), bf16[4,256,512]{2,1,0:T(8,128)(2,1)S(1)}, u32[]{:S(2)}, u32[]{:S(2)}) %all-to-all-start.9) | async-done | bytes 1048608 | tf_op jit(solution)/shard_map/all_to_all | solution.py:236
  (123 shorter events, 81.6 us)
Async XLA Ops:
  7.3 44.5 %all-to-all-start = ((bf16[8,2,2,48,512]{4,3,2,1,0:T(8,128)(2,1)}), bf16[8,2,2,48,512]{4,3,2,1,0:T(8,128)(2,1)}, u32[]{:S(2)}, u32[]{:S(2)}) async-start(bf16[8,2,2,48,512]{4,3,2,1,0:T(8,128)(2,1)} %copy-done.6), calls=%async_computation | async-start | bytes 3145728 | tf_op jit(solution)/shard_map/all_to_all | solution.py:162
  51.8 40.9 %all-to-all-start.2 = ((bf16[8,2,2,48,512]{4,3,2,1,0:T(8,128)(2,1)}), bf16[8,2,2,48,512]{4,3,2,1,0:T(8,128)(2,1)}, u32[]{:S(2)}, u32[]{:S(2)}) async-start(bf16[8,2,2,48,512]{4,3,2,1,0:T(8,128)(2,1)} %copy-done.5), calls=%async_computation.2 | async-start | bytes 3145728 | tf_op jit(solution)/shard_map/all_to_all | solution.py:162
  56.2 76.7 %collective-permute-start.1 = (bf16[8,2,2,48,512]{4,3,2,1,0:T(8,128)(2,1)}, bf16[8,2,2,48,512]{4,3,2,1,0:T(8,128)(2,1)}, u32[]{:S(2)}, u32[]{:S(2)}) collective-permute-start(bf16[8,2,2,48,512]{4,3,2,1,0:T(8,128)(2,1)} %all-to-all-done.refs_0_), channel_id=1, source_target_pairs={{0,2},{1,3},{2,0},{3,1},{4,6},{5,7},{6,4},{7,5},{8,10},{9,11},{10,... | collective-permute-start | bytes 4718600 | tf_op jit(solution)/shard_map/ppermute | solution.py:211
  92.8 46.0 %collective-permute-start.6 = (bf16[8,2,2,48,512]{4,3,2,1,0:T(8,128)(2,1)}, bf16[8,2,2,48,512]{4,3,2,1,0:T(8,128)(2,1)}, u32[]{:S(2)}, u32[]{:S(2)}) collective-permute-start(bf16[8,2,2,48,512]{4,3,2,1,0:T(8,128)(2,1)} %all-to-all-done.2.refs_0_), channel_id=1, source_target_pairs={{0,2},{1,3},{2,0},{3,1},{4,6},{5,7},{6,4},{7,5},{8,10},{9,11},{10,... | collective-permute-start | bytes 4718600 | tf_op jit(solution)/shard_map/ppermute | solution.py:211
  132.8 10.2 %collective-permute-start = (bf16[8,2,2,48,512]{4,3,2,1,0:T(8,128)(2,1)}, bf16[8,2,2,48,512]{4,3,2,1,0:T(8,128)(2,1)}, u32[]{:S(2)}, u32[]{:S(2)}) collective-permute-start(bf16[8,2,2,48,512]{4,3,2,1,0:T(8,128)(2,1)} %all-to-all-done.refs_0_), channel_id=1, source_target_pairs={{0,1},{1,0},{2,3},{3,2},{4,5},{5,4},{6,7},{7,6},{8,9},{9,8},{10,11... | collective-permute-start | bytes 4718600 | tf_op jit(solution)/shard_map/ppermute | solution.py:211
  132.9 10.2 %collective-permute-start.2 = (bf16[8,2,2,48,512]{4,3,2,1,0:T(8,128)(2,1)}, bf16[8,2,2,48,512]{4,3,2,1,0:T(8,128)(2,1)}, u32[]{:S(2)}, u32[]{:S(2)}) collective-permute-start(bf16[8,2,2,48,512]{4,3,2,1,0:T(8,128)(2,1)} %collective-permute-done.1.refs_2_), channel_id=1, source_target_pairs={{0,1},{1,0},{2,3},{3,2},{4,5},{5,4},{6,7},{7,6},{8,9},{9,8},{10,11... | collective-permute-start | bytes 4718600 | tf_op jit(solution)/shard_map/ppermute | solution.py:211
  138.6 39.3 %collective-permute-start.5 = (bf16[8,2,2,48,512]{4,3,2,1,0:T(8,128)(2,1)}, bf16[8,2,2,48,512]{4,3,2,1,0:T(8,128)(2,1)S(1)}, u32[]{:S(2)}, u32[]{:S(2)}) collective-permute-start(bf16[8,2,2,48,512]{4,3,2,1,0:T(8,128)(2,1)} %all-to-all-done.2.refs_0_), channel_id=1, source_target_pairs={{0,1},{1,0},{2,3},{3,2},{4,5},{5,4},{6,7},{7,6},{8,9},{9,8},{10,11... | collective-permute-start | bytes 4718600 | tf_op jit(solution)/shard_map/ppermute | solution.py:211
  138.8 39.2 %collective-permute-start.7 = (bf16[8,2,2,48,512]{4,3,2,1,0:T(8,128)(2,1)}, bf16[8,2,2,48,512]{4,3,2,1,0:T(8,128)(2,1)S(1)}, u32[]{:S(2)}, u32[]{:S(2)}) collective-permute-start(bf16[8,2,2,48,512]{4,3,2,1,0:T(8,128)(2,1)} %collective-permute-done.6.refs_2_), channel_id=1, source_target_pairs={{0,1},{1,0},{2,3},{3,2},{4,5},{5,4},{6,7},{7,6},{8,9},{9,8},{10,11... | collective-permute-start | bytes 4718600 | tf_op jit(solution)/shard_map/ppermute | solution.py:211
  143.1 67.4 %all-to-all-start.4 = ((bf16[8,2,2,32,512]{4,3,2,1,0:T(8,128)(2,1)}), bf16[8,2,2,32,512]{4,3,2,1,0:T(8,128)(2,1)}, u32[]{:S(2)}, u32[]{:S(2)}) async-start(bf16[8,2,2,32,512]{4,3,2,1,0:T(8,128)(2,1)} %shard_map.85), calls=%async_computation.4 | async-start | bytes 2097152 | tf_op jit(solution)/shard_map/all_to_all | solution.py:162
  177.8 33.2 %collective-permute-start.3 = (bf16[2,8,2,48,512]{4,3,2,1,0:T(8,128)(2,1)}, bf16[2,8,2,48,512]{4,3,2,1,0:T(8,128)(2,1)}, u32[]{:S(2)}, u32[]{:S(2)}) collective-permute-start(bf16[2,8,2,48,512]{4,3,2,1,0:T(8,128)(2,1)} %get-tuple-element.31), channel_id=1, source_target_pairs={{0,1},{1,0},{2,3},{3,2},{4,5},{5,4},{6,7},{7,6},{8,9},{9,8},{10,11... | collective-permute-start | bytes 4718600 | tf_op jit(solution)/shard_map/ppermute | solution.py:220
  179.6 31.4 %copy-start.11 = (f32[2,8,2,48,512]{4,3,2,1,0:T(8,128)S(1)}, f32[2,8,2,48,512]{4,3,2,1,0:T(8,128)}, u32[]{:S(2)}) copy-start(f32[2,8,2,48,512]{4,3,2,1,0:T(8,128)} %get-tuple-element.30) | copy-start | bytes 9437188
  210.0 26.8 %collective-permute-start.8 = (bf16[2,8,2,48,512]{4,3,2,1,0:T(8,128)(2,1)}, bf16[2,8,2,48,512]{4,3,2,1,0:T(8,128)(2,1)}, u32[]{:S(2)}, u32[]{:S(2)}) collective-permute-start(bf16[2,8,2,48,512]{4,3,2,1,0:T(8,128)(2,1)} %get-tuple-element.37), channel_id=1, source_target_pairs={{0,1},{1,0},{2,3},{3,2},{4,5},{5,4},{6,7},{7,6},{8,9},{9,8},{10,11... | collective-permute-start | bytes 4718600 | tf_op jit(solution)/shard_map/ppermute | solution.py:220
  210.5 26.3 %collective-permute-start.11 = (bf16[8,2,2,32,512]{4,3,2,1,0:T(8,128)(2,1)}, bf16[8,2,2,32,512]{4,3,2,1,0:T(8,128)(2,1)}, u32[]{:S(2)}, u32[]{:S(2)}) collective-permute-start(bf16[8,2,2,32,512]{4,3,2,1,0:T(8,128)(2,1)} %all-to-all-done.4.refs_0_), channel_id=1, source_target_pairs={{0,2},{1,3},{2,0},{3,1},{4,6},{5,7},{6,4},{7,5},{8,10},{9,11},{10,... | collective-permute-start | bytes 3145736 | tf_op jit(solution)/shard_map/ppermute | solution.py:211
  211.0 25.8 %copy-start.10 = (f32[2,8,2,48,512]{4,3,2,1,0:T(8,128)S(1)}, f32[2,8,2,48,512]{4,3,2,1,0:T(8,128)}, u32[]{:S(2)}) copy-start(f32[2,8,2,48,512]{4,3,2,1,0:T(8,128)} %get-tuple-element.36) | copy-start | bytes 9437188
  213.3 40.3 %collective-permute-start.4 = (bf16[1,8,2,48,512]{4,3,2,1,0:T(8,128)(2,1)S(1)}, bf16[1,8,2,48,512]{4,3,2,1,0:T(8,128)(2,1)S(1)}, u32[]{:S(2)}, u32[]{:S(2)}) collective-permute-start(bf16[1,8,2,48,512]{4,3,2,1,0:T(8,128)(2,1)S(1)} %slice.162), channel_id=1, source_target_pairs={{0,2},{1,3},{2,0},{3,1},{4,6},{5,7},{6,4},{7,5},{8,10},{9,11},{10,... | collective-permute-start | bytes 2359304 | tf_op jit(solution)/shard_map/ppermute | solution.py:220
  214.8 45.9 %collective-permute-start.10 = (bf16[8,2,2,32,512]{4,3,2,1,0:T(8,128)(2,1)}, bf16[8,2,2,32,512]{4,3,2,1,0:T(8,128)(2,1)}, u32[]{:S(2)}, u32[]{:S(2)}) collective-permute-start(bf16[8,2,2,32,512]{4,3,2,1,0:T(8,128)(2,1)} %all-to-all-done.4.refs_0_), channel_id=1, source_target_pairs={{0,1},{1,0},{2,3},{3,2},{4,5},{5,4},{6,7},{7,6},{8,9},{9,8},{10,11... | collective-permute-start | bytes 3145736 | tf_op jit(solution)/shard_map/ppermute | solution.py:211
  236.8 23.9 %collective-permute-start.12 = (bf16[8,2,2,32,512]{4,3,2,1,0:T(8,128)(2,1)}, bf16[8,2,2,32,512]{4,3,2,1,0:T(8,128)(2,1)}, u32[]{:S(2)}, u32[]{:S(2)}) collective-permute-start(bf16[8,2,2,32,512]{4,3,2,1,0:T(8,128)(2,1)} %collective-permute-done.11.refs_2_), channel_id=1, source_target_pairs={{0,1},{1,0},{2,3},{3,2},{4,5},{5,4},{6,7},{7,6},{8,9},{9,8},{10,11... | collective-permute-start | bytes 3145736 | tf_op jit(solution)/shard_map/ppermute | solution.py:211
  239.8 43.9 %collective-permute-start.9 = (bf16[1,8,2,48,512]{4,3,2,1,0:T(8,128)(2,1)}, bf16[1,8,2,48,512]{4,3,2,1,0:T(8,128)(2,1)}, u32[]{:S(2)}, u32[]{:S(2)}) collective-permute-start(bf16[1,8,2,48,512]{4,3,2,1,0:T(8,128)(2,1)} %slice.161), channel_id=1, source_target_pairs={{0,2},{1,3},{2,0},{3,1},{4,6},{5,7},{6,4},{7,5},{8,10},{9,11},{10,... | collective-permute-start | bytes 2359304 | tf_op jit(solution)/shard_map/ppermute | solution.py:220
  254.7 31.4 %all-to-all-start.1 = ((bf16[8,2,48,512]{3,2,1,0:T(8,128)(2,1)}), bf16[8,2,48,512]{3,2,1,0:T(8,128)(2,1)}, u32[]{:S(2)}, u32[]{:S(2)}) async-start(bf16[8,2,48,512]{3,2,1,0:T(8,128)(2,1)} %fusion.69), calls=%async_computation.1 | async-start | bytes 1572864 | tf_op jit(solution)/shard_map/all_to_all | solution.py:162
  283.7 8.4 %collective-permute-start.13 = (bf16[2,8,2,32,512]{4,3,2,1,0:T(8,128)(2,1)}, bf16[2,8,2,32,512]{4,3,2,1,0:T(8,128)(2,1)}, u32[]{:S(2)}, u32[]{:S(2)}) collective-permute-start(bf16[2,8,2,32,512]{4,3,2,1,0:T(8,128)(2,1)} %get-tuple-element.44), channel_id=1, source_target_pairs={{0,1},{1,0},{2,3},{3,2},{4,5},{5,4},{6,7},{7,6},{8,9},{9,8},{10,11... | collective-permute-start | bytes 3145736 | tf_op jit(solution)/shard_map/ppermute | solution.py:220
  286.1 26.8 %all-to-all-start.3 = ((bf16[8,2,48,512]{3,2,1,0:T(8,128)(2,1)}), bf16[8,2,48,512]{3,2,1,0:T(8,128)(2,1)S(1)}, u32[]{:S(2)}, u32[]{:S(2)}) async-start(bf16[8,2,48,512]{3,2,1,0:T(8,128)(2,1)} %fusion.70), calls=%async_computation.3 | async-start | bytes 1572864 | tf_op jit(solution)/shard_map/all_to_all | solution.py:162
  294.4 14.1 %collective-permute-start.14 = (bf16[1,8,2,32,512]{4,3,2,1,0:T(8,128)(2,1)S(1)}, bf16[1,8,2,32,512]{4,3,2,1,0:T(8,128)(2,1)S(1)}, u32[]{:S(2)}, u32[]{:S(2)}) collective-permute-start(bf16[1,8,2,32,512]{4,3,2,1,0:T(8,128)(2,1)S(1)} %slice.163), channel_id=1, source_target_pairs={{0,2},{1,3},{2,0},{3,1},{4,6},{5,7},{6,4},{7,5},{8,10},{9,11},{10,... | collective-permute-start | bytes 1572872 | tf_op jit(solution)/shard_map/ppermute | solution.py:220
  300.2 32.3 %collective-permute-start.15 = (bf16[1024,512]{1,0:T(8,128)(2,1)S(1)}, bf16[1024,512]{1,0:T(8,128)(2,1)S(1)}, u32[]{:S(2)}, u32[]{:S(2)}) collective-permute-start(bf16[1024,512]{1,0:T(8,128)(2,1)S(1)} %fusion.47), channel_id=1, source_target_pairs={{0,4},{4,0},{8,12},{12,8},{16,20},{20,16},{24,28},{28,24},{1,5},{5... | collective-permute-start | bytes 3145736 | tf_op jit(solution)/shard_map/ppermute | solution.py:233
  312.9 20.9 %all-to-all-start.5 = ((bf16[8,2,32,512]{3,2,1,0:T(8,128)(2,1)}), bf16[8,2,32,512]{3,2,1,0:T(8,128)(2,1)S(1)}, u32[]{:S(2)}, u32[]{:S(2)}) async-start(bf16[8,2,32,512]{3,2,1,0:T(8,128)(2,1)} %fusion.71), calls=%async_computation.5 | async-start | bytes 1048576 | tf_op jit(solution)/shard_map/all_to_all | solution.py:162
  333.8 35.6 %all-to-all-start.6 = ((bf16[4,256,512]{2,1,0:T(8,128)(2,1)}), bf16[4,256,512]{2,1,0:T(8,128)(2,1)S(1)}, u32[]{:S(2)}, u32[]{:S(2)}) async-start(bf16[4,256,512]{2,1,0:T(8,128)(2,1)} %bitcast.24), calls=%async_computation.6 | async-start | bytes 2097152 | tf_op jit(solution)/shard_map/all_to_all | solution.py:236
  343.7 24.4 %collective-permute-start.16 = (bf16[1024,512]{1,0:T(8,128)(2,1)S(1)}, bf16[1024,512]{1,0:T(8,128)(2,1)S(1)}, u32[]{:S(2)}, u32[]{:S(2)}) collective-permute-start(bf16[1024,512]{1,0:T(8,128)(2,1)S(1)} %fusion.52), channel_id=1, source_target_pairs={{0,4},{4,0},{8,12},{12,8},{16,20},{20,16},{24,28},{28,24},{1,5},{5... | collective-permute-start | bytes 3145736 | tf_op jit(solution)/shard_map/ppermute | solution.py:233
  369.4 34.3 %all-to-all-start.7 = ((bf16[4,256,512]{2,1,0:T(8,128)(2,1)}), bf16[4,256,512]{2,1,0:T(8,128)(2,1)}, u32[]{:S(2)}, u32[]{:S(2)}) async-start(bf16[4,256,512]{2,1,0:T(8,128)(2,1)} %bitcast.26), calls=%async_computation.7 | async-start | bytes 2097152 | tf_op jit(solution)/shard_map/all_to_all | solution.py:236
  379.5 22.9 %collective-permute-start.17 = (bf16[1024,512]{1,0:T(8,128)(2,1)S(1)}, bf16[1024,512]{1,0:T(8,128)(2,1)S(1)}, u32[]{:S(2)}, u32[]{:S(2)}) collective-permute-start(bf16[1024,512]{1,0:T(8,128)(2,1)S(1)} %fusion.57), channel_id=1, source_target_pairs={{0,4},{4,0},{8,12},{12,8},{16,20},{20,16},{24,28},{28,24},{1,5},{5... | collective-permute-start | bytes 3145736 | tf_op jit(solution)/shard_map/ppermute | solution.py:233
  385.0 23.7 %copy-start.7 = (bf16[2048,512]{1,0:T(8,128)(2,1)S(1)}, bf16[2048,512]{1,0:T(8,128)(2,1)}, u32[]{:S(2)}) copy-start(bf16[2048,512]{1,0:T(8,128)(2,1)} %get-tuple-element.48) | copy-start | bytes 6291460
  403.7 32.4 %all-to-all-start.8 = ((bf16[4,256,512]{2,1,0:T(8,128)(2,1)}), bf16[4,256,512]{2,1,0:T(8,128)(2,1)}, u32[]{:S(2)}, u32[]{:S(2)}) async-start(bf16[4,256,512]{2,1,0:T(8,128)(2,1)} %bitcast.28), calls=%async_computation.8 | async-start | bytes 2097152 | tf_op jit(solution)/shard_map/all_to_all | solution.py:236
  413.3 21.5 %collective-permute-start.18 = (bf16[1024,512]{1,0:T(8,128)(2,1)S(1)}, bf16[1024,512]{1,0:T(8,128)(2,1)S(1)}, u32[]{:S(2)}, u32[]{:S(2)}) collective-permute-start(bf16[1024,512]{1,0:T(8,128)(2,1)S(1)} %fusion.65), channel_id=1, source_target_pairs={{0,4},{4,0},{8,12},{12,8},{16,20},{20,16},{24,28},{28,24},{1,5},{5... | collective-permute-start | bytes 3145736 | tf_op jit(solution)/shard_map/ppermute | solution.py:233
  436.1 26.1 %all-to-all-start.9 = ((bf16[4,256,512]{2,1,0:T(8,128)(2,1)}), bf16[4,256,512]{2,1,0:T(8,128)(2,1)S(1)}, u32[]{:S(2)}, u32[]{:S(2)}) async-start(bf16[4,256,512]{2,1,0:T(8,128)(2,1)} %bitcast.32), calls=%async_computation.9 | async-start | bytes 2097152 | tf_op jit(solution)/shard_map/all_to_all | solution.py:236
  (16 other events, 91.4 us)
